TPU v7x, 32 devices: a whole 2x2x4 slice. The times are simulated.
32 devices in a mesh: groups: 2 (over x), mp: 16 (over z, y, core).
Axes of the slice: x: 2, y: 2, z: 4, core: 2. Of those that a mesh axis runs over, the one named last changes fastest.
Arguments:
- stream: bfloat16 [256, 12288], P('groups', 'mp'), parts along dimension 0
- target_ids: int32 [256], P('groups'), parts along dimension 0, may hold values from 0 to 4095
- lengths: int32 [4], P('groups'), parts along dimension 0, may hold values from 1 to 64, as said below
- attn_gain: float32 [12288], replicated, may hold values from 0.1 to 1.9
- w_query: bfloat16 [12288, 2048], P(None, 'mp')
- w_key: bfloat16 [12288, 1024], P(None, 'mp')
- w_value: bfloat16 [12288, 1024], P(None, 'mp'), may hold values from -0.0546875 to 0.0546875
- w_out: bfloat16 [2048, 12288], P('mp'), may hold values from -0.125 to 0.125
- final_gain: float32 [12288], replicated, may hold values from 0.1 to 1.9
- lm_head: bfloat16 [12288, 4096], P(None, 'mp')
Outputs:
- layer_out: bfloat16 [256, 12288], P('groups', 'mp'), parts along dimension 0
- token_logprob: float32 [256], P('groups'), parts along dimension 0
There are 2 independent parts, one for each index of `groups`. A program takes and returns all parts, laid end to end along the dimension named above; an argument that names none is the same for every part. Nothing has to cross between parts.
Inputs may be any that keep to these rules, and one draw needn't show every extreme that they name: `lengths`: one slot has length 64.
All inputs are finite; a program needn't handle non-finite values.
Results may differ from a plain program's by a relative error of at most 0.0068.
Values may be sent and summed in bfloat16 or wider, within the bound.
A program may use at most 64 MiB of HBM per device.

v0:
```python
import jax
import jax.numpy as jnp
from jax import lax
from jax.sharding import PartitionSpec as P

D = 12288
KVH = 8
HD = 128
SEQS = 2


def rotate(values, positions, first_col):
    rows, cols = values.shape
    pairs = jnp.arange(cols // 2, dtype=jnp.int32)
    within = (first_col + 2 * pairs) % HD
    freq = jnp.power(jnp.float32(1000000.0), -within.astype(jnp.float32) / HD)
    angle = positions.astype(jnp.float32)[:, None] * freq[None, :]
    cosine = jnp.cos(angle)
    sine = jnp.sin(angle)
    paired = values.reshape(rows, cols // 2, 2)
    first = paired[:, :, 0]
    second = paired[:, :, 1]
    turned = jnp.stack([first * cosine - second * sine, first * sine + second * cosine], axis=-1)
    return turned.reshape(rows, cols)


def scaled_local(values, total, gain_part):
    scale = lax.rsqrt(total / D + 1e-05)
    return (values.astype(jnp.float32) * scale[:, None] * gain_part[None, :]).astype(jnp.bfloat16)


def body(
    stream, target_ids, lengths, attn_gain, w_query, w_key, w_value, w_out, final_gain, lm_head
):
    rank = lax.axis_index("mp")
    tokens = stream.shape[0]
    width = stream.shape[1]
    seq_len = tokens // SEQS
    head_dim = w_query.shape[1]
    kv_cols = w_key.shape[1]
    voc_dev = lm_head.shape[1]
    attn_part = lax.dynamic_slice_in_dim(attn_gain, rank * width, width, 0)
    final_part = lax.dynamic_slice_in_dim(final_gain, rank * width, width, 0)
    wide = stream.astype(jnp.float32)
    sum_sq = lax.psum(jnp.sum(wide * wide, axis=1), "mp")
    normed_local = scaled_local(stream, sum_sq, attn_part)
    piece = lax.all_gather(normed_local, "mp", axis=1, tiled=True)
    q_full = jnp.dot(piece, w_query, preferred_element_type=jnp.float32)
    k_full = jnp.dot(piece, w_key, preferred_element_type=jnp.float32)
    v_full = jnp.dot(piece, w_value, preferred_element_type=jnp.float32)
    rows = jnp.arange(tokens, dtype=jnp.int32)
    positions = rows % seq_len
    slots = rows // seq_len
    query = rotate(q_full, positions, rank * head_dim).astype(jnp.bfloat16)
    key_local = rotate(k_full, positions, rank * kv_cols).astype(jnp.bfloat16)
    value_local = v_full.astype(jnp.bfloat16)
    keys, values = (
        lax.all_gather(key_local, "mp", axis=1, tiled=True),
        lax.all_gather(value_local, "mp", axis=1, tiled=True),
    )
    kv_head = rank % KVH
    key_head = lax.dynamic_slice_in_dim(keys, kv_head * head_dim, head_dim, 1)
    value_head = lax.dynamic_slice_in_dim(values, kv_head * head_dim, head_dim, 1)
    slot_len = jnp.sum(
        jnp.where(
            slots[:, None] == jnp.arange(SEQS, dtype=jnp.int32)[None, :], lengths[None, :], 0
        ),
        axis=1,
    )
    visible = (
        (slots[None, :] == slots[:, None])
        & (positions[None, :] <= positions[:, None])
        & (positions[None, :] < slot_len[None, :])
    )
    scores = jnp.dot(query, key_head.T, preferred_element_type=jnp.float32) / jnp.sqrt(
        jnp.float32(head_dim)
    )
    scores = jnp.where(visible, scores, jnp.float32(-1e30))
    top_score = jnp.max(scores, axis=1, keepdims=True)
    weights = jnp.exp(scores - top_score)
    probs = (weights / jnp.sum(weights, axis=1, keepdims=True)).astype(jnp.bfloat16)
    attn = jnp.dot(probs, value_head, preferred_element_type=jnp.float32).astype(jnp.bfloat16)
    summed_cols = lax.psum_scatter(
        lax.dot_general(w_out, attn, (((0,), (1,)), ((), ())), preferred_element_type=jnp.float32),
        "mp",
        scatter_dimension=0,
        tiled=True,
    )
    layer_out = (stream.astype(jnp.float32) + summed_cols.T).astype(jnp.bfloat16)
    layer_wide = layer_out.astype(jnp.float32)
    layer_sq = lax.psum(jnp.sum(layer_wide * layer_wide, axis=1), "mp")
    final_local = scaled_local(layer_out, layer_sq, final_part)
    logits = jnp.dot(
        lax.all_gather(final_local, "mp", axis=1, tiled=True),
        lm_head,
        preferred_element_type=jnp.float32,
    )
    local_ids = target_ids - rank * voc_dev
    hits = jnp.arange(voc_dev, dtype=jnp.int32)[None, :] == local_ids[:, None]
    picked_part = jnp.sum(jnp.where(hits, logits, 0.0), axis=1)
    part_max = jnp.max(logits, axis=1)
    top = lax.pmax(part_max, "mp")
    total, picked = lax.psum((jnp.sum(jnp.exp(logits - top[:, None]), axis=1), picked_part), "mp")
    token_logprob = picked - top - jnp.log(total)
    return (layer_out, token_logprob)


def solution(mesh):
    return jax.shard_map(
        body,
        mesh=mesh,
        in_specs=(
            P("groups", "mp"),
            P("groups"),
            P("groups"),
            P(),
            P(None, "mp"),
            P(None, "mp"),
            P(None, "mp"),
            P("mp", None),
            P(),
            P(None, "mp"),
        ),
        out_specs=(P("groups", "mp"), P("groups")),
        check_vma=False,
    )
```

profile of v0, /device:TPU:0, one launch (start us, length us, event | category | flops | bytes accessed | tf_op | source)
XLA Modules:
  0.0 372.2 jit_solution(17327716938286548073)
XLA Ops:
  7.2 0.0 all-gather.3.cloned.1.call-start
  7.2 1.2 fusion.4
  8.4 34.9 %psum.28 = f32[128]{0:T(128)S(1)} all-reduce(f32[128]{0:T(128)S(1)} %fusion.4), channel_id=1, replica_groups=mesh['groups'=2,'mp'=16] {'mp'}, use_global_device_ids=true, to_apply=%region_2.3 | all-reduce | flops 128 | bytes 1024 | tf_op jit(solution)/shard_map/psum | solution.py:45
  43.4 0.8 dynamic_slice.12
  44.1 1.7 fusion.6
  45.8 0.0 all-gather.3.cloned.1.call-update
  45.9 0.0 reduce-scatter.2.cloned.1.call-start
  46.0 0.7 fusion.32
  46.8 42.2 %all-gather.3.cloned.1.call-done = bf16[128,12288]{1,0:T(8,128)(2,1)} async-done(((bf16[128,768]{1,0:T(8,128)(2,1)}), bf16[128,12288]{1,0:T(8,128)(2,1)}) %all-gather.3.cloned.1.call-update) | async-done | bytes 3145744 | tf_op jit(solution)/shard_map/all_gather | solution.py:47
  88.9 3.7 fusion.54
  92.7 0.1 fusion.29
  92.8 19.6 %all_gather.13 = bf16[128,1024]{0,1:T(8,128)(2,1)S(1)} all-gather(bf16[128,64]{0,1:T(8,128)(2,1)S(1)} %bitcast.27), channel_id=1, replica_groups=mesh['groups'=2,'mp'=16] {'mp'}, dimensions={1}, use_global_device_ids=true | all-gather | bytes 278528 | tf_op jit(solution)/shard_map/all_gather | solution.py:58
  112.4 3.3 fusion.53
  115.8 0.1 fusion.49
  115.8 0.2 fusion.14
  116.1 1.2 convolution_convert_fusion.1
  117.3 18.2 %all_gather.14 = bf16[128,1024]{0,1:T(8,128)(2,1)S(1)} all-gather(bf16[128,64]{0,1:T(8,128)(2,1)S(1)} %convolution_convert_fusion.1), channel_id=1, replica_groups=mesh['groups'=2,'mp'=16] {'mp'}, dimensions={1}, use_global_device_ids=true | all-gather | bytes 278528 | tf_op jit(solution)/shard_map/all_gather | solution.py:59
  135.5 0.2 fusion.51
  135.7 3.8 %convolution_bitcast_fusion = f32[12288,128]{0,1:T(8,128)} fusion(bf16[128,12288]{1,0:T(8,128)(2,1)S(1)} %copy-done, f32[128,128]{0,1:T(8,128)S(1)} %get-tuple-element.17, bf16[128,1024]{0,1:T(8,128)(2,1)S(1)} %all_gather.14, s32[]{:T(128)S(6)} %select_n.95, f32[128]{0:T(128)S(1)} %fusion.8, f32[128]{0:T(128)S(1)} %get-tuple-element.16), kind=kOutput, calls=%fused_computation | convolution fusion | flops 406913024 | bytes 9536516 | tf_op jit(solution)/shard_map/dot_general | solution.py:84
  139.6 0.0 reduce-scatter.2.cloned.1.call-update
  139.6 0.0 all-gather.5.cloned.1.call-start
  139.6 0.8 dynamic_slice.15
  140.4 82.9 %reduce-scatter.2.cloned.1.call-done = f32[768,128]{0,1:T(8,128)} async-done(((f32[12288,128]{0,1:T(8,128)}), f32[768,128]{0,1:T(8,128)}) %reduce-scatter.2.cloned.1.call-update) | async-done | bytes 393232 | tf_op jit(solution)/shard_map/reduce_scatter | solution.py:83
  223.3 1.1 fusion.1
  224.5 31.2 %psum.29 = f32[128]{0:T(128)S(1)} all-reduce(f32[128]{0:T(128)S(1)} %get-tuple-element.6), channel_id=1, replica_groups=mesh['groups'=2,'mp'=16] {'mp'}, use_global_device_ids=true, to_apply=%region_7.8 | all-reduce | flops 128 | bytes 1024 | tf_op jit(solution)/shard_map/psum | solution.py:91
  255.7 0.8 fusion.3
  256.6 43.0 %all-gather.5.cloned.1.call-done = bf16[128,12288]{1,0:T(8,128)(2,1)} async-done(((bf16[128,768]{1,0:T(8,128)(2,1)}), bf16[128,12288]{1,0:T(8,128)(2,1)}) %all-gather.5.cloned.1.call-update) | async-done | bytes 3145744 | tf_op jit(solution)/shard_map/all_gather | solution.py:94
  299.5 4.8 %fusion.52 = (f32[128]{0:T(128)S(1)}, f32[128,256]{1,0:T(8,128)S(1)}) fusion(bf16[128,12288]{1,0:T(8,128)(2,1)} %all-gather.5.cloned.1.call-done, bf16[12288,256]{1,0:T(8,128)(2,1)} %param.19), kind=kOutput, calls=%fused_computation.83 | convolution fusion | flops 805339008 | bytes 9568768 | tf_op jit(solution)/shard_map/dot_general | solution.py:93
  304.4 31.1 %pmax.7 = f32[128]{0:T(128)S(1)} all-reduce(f32[128]{0:T(128)S(1)} %get-tuple-element.18), channel_id=1, replica_groups=mesh['groups'=2,'mp'=16] {'mp'}, use_global_device_ids=true, to_apply=%region_11.12 | all-reduce | flops 128 | bytes 1024 | tf_op jit(solution)/shard_map/pmax | solution.py:102
  335.5 0.2 select_reduce_fusion
  335.7 29.5 %all-reduce = (f32[128]{0:T(128)S(1)}, f32[128]{0:T(128)S(1)}) all-reduce(f32[128]{0:T(128)S(1)} %get-tuple-element.3, f32[128]{0:T(128)S(1)} %get-tuple-element.2), channel_id=1, replica_groups=mesh['groups'=2,'mp'=16] {'mp'}, use_global_device_ids=true, to_apply=%region_13.14 | all-reduce | flops 256 | bytes 2048 | tf_op jit(solution)/shard_map/psum | solution.py:103
  365.2 0.5 log_subtract_fusion
  (27 shorter events, 0.3 us)
Async XLA Ops:
  7.2 128.6 %copy-start = (bf16[128,12288]{1,0:T(8,128)(2,1)S(1)}, bf16[128,12288]{1,0:T(8,128)(2,1)}, u32[]{:S(2)}) copy-start(bf16[128,12288]{1,0:T(8,128)(2,1)} %param.17) | copy-start | bytes 9437188
  7.2 81.7 %all-gather.3.cloned.1.call-start = ((), (), s32[]{:S(2)}) async-start(), calls=%async_computation.1 | async-start | bytes 3342336 | tf_op jit(solution)/shard_map/all_gather | solution.py:47
  45.9 177.5 %reduce-scatter.2.cloned.1.call-start = ((), (), s32[]{:S(2)}) async-start(), calls=%async_computation.2 | async-start | bytes 6684672 | tf_op jit(solution)/shard_map/reduce_scatter | solution.py:83
  88.9 23.5 %copy-start.1 = (bf16[128,12288]{1,0:T(8,128)(2,1)S(1)}, bf16[128,12288]{1,0:T(8,128)(2,1)}, u32[]{:S(2)}) copy-start(bf16[128,12288]{1,0:T(8,128)(2,1)} %all-gather.3.cloned.1.call-done) | copy-start | bytes 9437188
  112.4 3.7 copy-start.3
  139.6 83.8 %copy-start.2 = (bf16[128,768]{1,0:T(8,128)(2,1)S(1)}, bf16[128,768]{1,0:T(8,128)(2,1)}, u32[]{:S(2)}) copy-start(bf16[128,768]{1,0:T(8,128)(2,1)} %param.10) | copy-start | bytes 589828
  139.6 117.0 %copy-start.5 = (s32[128]{0:T(128)S(1)}, s32[128]{0:T(128)}, u32[]{:S(2)}) copy-start(s32[128]{0:T(128)} %param.11) | copy-start | bytes 1540
  139.6 160.0 %all-gather.5.cloned.1.call-start = ((), (), s32[]{:S(2)}) async-start(), calls=%async_computation.3 | async-start | bytes 3342336 | tf_op jit(solution)/shard_map/all_gather | solution.py:94
  224.5 79.9 %copy-start.4 = (bf16[128,768]{1,0:T(8,128)(2,1)}, bf16[128,768]{1,0:T(8,128)(2,1)S(1)}, u32[]{:S(2)}) copy-start(bf16[128,768]{1,0:T(8,128)(2,1)S(1)} %get-tuple-element.7) | copy-start | bytes 589828
Sparse Core Ops, SparseCore 0:
  46.0 42.8 all-gather.2
  139.7 83.5 reduce-scatter.1
  256.7 42.8 all-gather.4
where the time goes:
time: 373 us; the launch traced here: 372 us
  waiting for transfers between devices  168 us (45%)
  blocking collectives  164 us (44%)
  matrix products  17.1 us (5%)
  between operations  13.9 us (4%)
  other arithmetic  6.78 us (2%)
    reduce_scatter x1, waiting for transfers between devices, body(): lax.psum_scatter(lax.dot_general(w_out, attn, (((0,), (1,)), ((), ())), p...  82.9 us
    all_gather x1, waiting for transfers between devices, body(): lax.all_gather(final_local, 'mp', axis=1, tiled=True)  43 us
    all_gather x1, waiting for transfers between devices, body(): piece = lax.all_gather(normed_local, 'mp', axis=1, tiled=True)  42.2 us
    psum x1, blocking collectives, body(): sum_sq = lax.psum(jnp.sum(wide * wide, axis=1), 'mp')  34.9 us
    psum x1, blocking collectives, body(): layer_sq = lax.psum(jnp.sum(layer_wide * layer_wide, axis=1), 'mp')  31.2 us
    pmax x1, blocking collectives, body(): top = lax.pmax(part_max, 'mp')  31.1 us
    psum x1, blocking collectives, body(): lax.psum((jnp.sum(jnp.exp(logits - top[:, None]), axis=1), picked_part),...  29.5 us
    all_gather x1, blocking collectives, body(): lax.all_gather(key_local, 'mp', axis=1, tiled=True)  19.6 us
  transfers between devices with their start and end apart: 3, of which 3 were waited for; matrix products, arithmetic and copies ran while one was open for 0% of the time, Pallas kernels for 0%

commit v1 on v0

v1 whole, which is shorter than its diff:
```python
import functools

import jax
import jax.numpy as jnp
import numpy as np
from jax import lax
from jax.experimental import pallas as pl
from jax.experimental.pallas import tpu as pltpu
from jax.sharding import PartitionSpec as P

KVH = 8
HD = 128
SEQS = 2
B, C = 2, 2
BF16, F32 = jnp.bfloat16, jnp.float32


def rope_tables(tokens):
    positions = (np.arange(tokens) % (tokens // SEQS)).astype(np.float32)
    within = 2 * (np.arange(HD) // 2)
    freq = np.power(np.float32(1000000.0), -within.astype(np.float32) / np.float32(HD))
    angle = (positions[:, None] * freq[None, :].astype(np.float32)).astype(np.float32)
    sine = np.sin(angle.astype(np.float64))
    sine = np.where(np.arange(HD)[None, :] % 2 == 0, -sine, sine)
    return np.cos(angle.astype(np.float64)).astype(np.float32), sine.astype(np.float32)


def rope(values, cosine, sine):
    even = lax.broadcasted_iota(jnp.int32, values.shape, 1) % 2 == 0
    swapped = jnp.where(even, pltpu.roll(values, HD - 1, 1), pltpu.roll(values, 1, 1))
    return values * cosine + swapped * sine


def kernel(
    n, depth,
    x_ref, ids_ref, len_ref, gain1_ref, gain2_ref, cos_ref, sin_ref,
    wq_hbm, wk_hbm, wv_hbm, wo_hbm, lm_hbm,
    out_ref, logp_ref,
    wq, wk, wv, wo, lm, X1, X2, acc_q, acc_k, acc_v, ssq, acc_l,
    kvs, kvr, attn, cs, cr, ys, yr, us, ur, ds, dr, tot, st,
    wsem, wosem, ag_s1, ag_r1, ag_s2, ag_r2, kv_s, kv_r,
    cs_s, cs_r, ys_s, ys_r, us_s, us_r, ds_s, ds_r, st_s, st_r,
):
    A = n // (B * C)
    me = lax.axis_index("mp")
    c = lax.rem(me, C)
    y = lax.rem(lax.div(me, C), B)
    z = lax.div(me, B * C)
    tokens, width = x_ref.shape
    kv_cols = wk.shape[2]
    pieces = HD // kv_cols
    users = n // KVH

    def idx(zz, yy, cc):
        return (zz * B + yy) * C + cc

    core, side = idx(z, y, 1 - c), idx(z, 1 - y, c)
    above, below = idx(z + 1, y, c), idx(z - 1, y, c)

    def rc(src, dst, ssem, rsem, dev):
        return pltpu.make_async_remote_copy(
            src_ref=src, dst_ref=dst, send_sem=ssem, recv_sem=rsem,
            device_id={"mp": dev}, device_id_type=pl.DeviceIdType.MESH,
        )

    loads = [
        pltpu.make_async_copy(src, dst, wsem.at[i])
        for i, (src, dst) in enumerate(((wq_hbm, wq), (wk_hbm, wk), (wv_hbm, wv), (lm_hbm, lm)))
    ]

    def wo_load(j):
        src = wo_hbm.at[j] if len(wo_hbm.shape) == 3 else wo_hbm.at[:, j * width:(j + 1) * width]
        return pltpu.make_async_copy(src, wo.at[j], wosem.at[j])

    barrier = pltpu.get_barrier_semaphore()

    def greet(i, carry):
        pl.semaphore_signal(
            barrier, inc=1, device_id={"mp": lax.rem(me + i, n)}, device_id_type=pl.DeviceIdType.MESH
        )
        return carry

    lax.fori_loop(1, n, greet, 0)
    for load in loads[:3]:
        load.start()
    X1[me] = x_ref[...]
    acc_q[...] = jnp.zeros_like(acc_q)
    acc_k[...] = jnp.zeros_like(acc_k)
    acc_v[...] = jnp.zeros_like(acc_v)
    acc_l[...] = jnp.zeros_like(acc_l)
    ssq[...] = jnp.zeros_like(ssq)
    pl.semaphore_wait(barrier, n - 1)

    def gather(X, ss, rs, consume, prepare):
        def send(slot, kind, k, dev):
            return rc(X.at[slot], X.at[slot], ss.at[kind, k], rs.at[slot], dev)

        def got(slot):
            rc(X.at[slot], X.at[slot], ss.at[0, 0], rs.at[slot], core).wait_recv()

        @pl.when(z < A - 1)
        def _():
            send(me, 0, z, above).start()

        @pl.when(z > 0)
        def _():
            send(me, 1, z, below).start()

        send(me, 2, z, side).start()
        send(me, 3, z * B + y, core).start()
        prepare()
        consume(me)

        def valid(k, g, zz):
            return (k >= 0) & (k < A) & (zz >= 0) & (zz < A) & ((k > 0) | (g == 0))

        def step(s, carry):
            def line(g, carry):
                zz = z + (2 * g - 1) * s

                @pl.when(valid(s, g, zz))
                def _():
                    slot = idx(zz, y, c)
                    got(slot)

                    @pl.when((g == 0) & (z < A - 1))
                    def _():
                        send(slot, 0, zz, above).start()

                    @pl.when((g == 1) & (z > 0))
                    def _():
                        send(slot, 1, zz, below).start()

                    send(slot, 2, zz, side).start()
                    send(slot, 3, zz * B + y, core).start()

                return carry

            lax.fori_loop(0, 2, line, 0)

            def line_use(g, carry):
                zz = z + (2 * g - 1) * s

                @pl.when(valid(s, g, zz))
                def _():
                    consume(idx(zz, y, c))

                return carry

            lax.fori_loop(0, 2, line_use, 0)

            def across(g, carry):
                zz = z + (2 * g - 1) * (s - 1)

                @pl.when(valid(s - 1, g, zz))
                def _():
                    slot = idx(zz, 1 - y, c)
                    got(slot)
                    send(slot, 3, zz * B + 1 - y, core).start()
                    consume(slot)
                    slot2 = idx(zz, y, 1 - c)
                    got(slot2)
                    consume(slot2)

                return carry

            lax.fori_loop(0, 2, across, 0)

            def last(g, carry):
                zz = z + (2 * g - 1) * (s - 2)

                @pl.when(valid(s - 2, g, zz))
                def _():
                    slot = idx(zz, 1 - y, 1 - c)
                    got(slot)
                    consume(slot)

                return carry

            lax.fori_loop(0, 2, last, 0)
            return carry

        lax.fori_loop(1, A + 2, step, 0)

        def drain(zz, carry):
            slot = idx(zz, y, c)

            @pl.when((zz <= z) & (z < A - 1))
            def _():
                send(slot, 0, zz, above).wait_send()

            @pl.when((zz >= z) & (z > 0))
            def _():
                send(slot, 1, zz, below).wait_send()

            send(slot, 2, zz, side).wait_send()
            send(slot, 3, zz * B + y, core).wait_send()
            other = idx(zz, 1 - y, c)
            send(other, 3, zz * B + 1 - y, core).wait_send()
            return carry

        return lambda: lax.fori_loop(0, A, drain, 0)

    def project(slot):
        wide = X1[slot].astype(F32)
        ssq[...] += jnp.sum(wide * wide, axis=1, keepdims=True)
        piece = (wide * gain1_ref[slot]).astype(BF16)
        acc_q[...] += jnp.dot(piece, wq[slot], preferred_element_type=F32)
        acc_k[...] += jnp.dot(piece, wk[slot], preferred_element_type=F32)
        acc_v[...] += jnp.dot(piece, wv[slot], preferred_element_type=F32)

    def ready():
        for load in loads[:3]:
            load.wait()
        for j in range(n):
            wo_load(j).start()
        loads[3].start()

    drain1 = gather(X1, ag_s1, ag_r1, project, ready)

    scale = lax.rsqrt(ssq[...] / depth + 1e-05)
    kvs[0] = acc_k[...] * scale
    kvs[1] = acc_v[...] * scale
    piece_id, head_of = lax.rem(me, pieces), lax.div(me, pieces)

    def kv_send(i):
        return rc(kvs, kvr.at[piece_id], kv_s.at[i], kv_r.at[piece_id], head_of + KVH * i)

    for i in range(users):
        @pl.when(head_of + KVH * i != me)
        def _():
            kv_send(i).start()

        @pl.when(head_of + KVH * i == me)
        def _():
            kvr[piece_id] = kvs[...]

    cosine, sine = cos_ref[...], sin_ref[...]
    query = rope(acc_q[...] * scale, cosine, sine).astype(BF16)
    source = lax.rem(me, KVH) * pieces
    for i in range(pieces):
        @pl.when(source + i != me)
        def _():
            rc(kvs, kvr.at[i], kv_s.at[0], kv_r.at[i], core).wait_recv()

    key = jnp.concatenate([kvr[i, 0] for i in range(pieces)], axis=1)
    key = rope(key, cosine, sine).astype(BF16)
    value = jnp.concatenate([kvr[i, 1] for i in range(pieces)], axis=1).astype(BF16)
    seq_len = tokens // SEQS
    row = lax.broadcasted_iota(jnp.int32, (tokens, tokens), 0)
    col = lax.broadcasted_iota(jnp.int32, (tokens, tokens), 1)
    limit = jnp.full((tokens, tokens), len_ref[0], jnp.int32)
    for i in range(1, SEQS):
        limit = jnp.where(col >= i * seq_len, len_ref[i], limit)
    visible = (row // seq_len == col // seq_len) & (col <= row) & (col % seq_len < limit)
    scores = lax.dot_general(query, key, (((1,), (1,)), ((), ())), preferred_element_type=F32)
    scores = jnp.where(visible, scores / np.float32(np.sqrt(HD)), jnp.float32(-1e30))
    weights = jnp.exp(scores - jnp.max(scores, axis=1, keepdims=True))
    probs = (weights / jnp.sum(weights, axis=1, keepdims=True)).astype(BF16)
    attn[...] = jnp.dot(probs, value, preferred_element_type=F32).astype(BF16)
    for j in range(n):
        wo_load(j).wait()

    def partial(slot):
        return jnp.dot(attn[...], wo[slot], preferred_element_type=F32)

    def far_first(body):
        def step(i, carry):
            s = A - 1 - lax.div(i, 2)
            zz = z + (1 - 2 * lax.rem(i, 2)) * s

            @pl.when((zz >= 0) & (zz < A) & ((s > 0) | (lax.rem(i, 2) == 0)))
            def _():
                body(zz)

            return carry

        lax.fori_loop(0, 2 * A, step, 0)

    def core_copy(yy, zz):
        return rc(cs.at[yy, zz], cr.at[yy, zz], cs_s.at[yy, zz], cs_r.at[yy, zz], core)

    def to_core(yy):
        def body(zz):
            cs[yy, zz] = partial(idx(zz, yy, 1 - c)).astype(BF16)
            core_copy(yy, zz).start()

        return body

    def side_copy(zz):
        return rc(ys.at[zz], yr.at[zz], ys_s.at[zz], ys_r.at[zz], side)

    def to_side(zz):
        total = partial(idx(zz, 1 - y, c))
        core_copy(1 - y, zz).wait_recv()
        ys[zz] = (total + cr[1 - y, zz].astype(F32)).astype(BF16)
        side_copy(zz).start()

    def up_copy(zz):
        return rc(us.at[zz], ur.at[zz], us_s.at[zz], us_r.at[zz], above)

    def down_copy(zz):
        return rc(ds.at[zz], dr.at[zz], ds_s.at[zz], ds_r.at[zz], below)

    def both(zz):
        to_core(1 - y)(zz)

    far_first(both)
    far_first(to_side)
    far_first(lambda zz: to_core(y)(zz))

    def along(zz):
        total = partial(idx(zz, y, c))
        core_copy(y, zz).wait_recv()
        total += cr[y, zz].astype(F32)
        side_copy(zz).wait_recv()
        acc = total + yr[zz].astype(F32)

        @pl.when(zz > z)
        def _():
            @pl.when(z > 0)
            def _():
                up_copy(zz).wait_recv()
                us[zz] = (acc + ur[zz].astype(F32)).astype(BF16)

            @pl.when(z == 0)
            def _():
                us[zz] = acc.astype(BF16)

            up_copy(zz).start()

        @pl.when(zz < z)
        def _():
            @pl.when(z < A - 1)
            def _():
                down_copy(zz).wait_recv()
                ds[zz] = (acc + dr[zz].astype(F32)).astype(BF16)

            @pl.when(z == A - 1)
            def _():
                ds[zz] = acc.astype(BF16)

            down_copy(zz).start()

        @pl.when(zz == z)
        def _():
            tot[...] = acc

            @pl.when(z > 0)
            def _():
                up_copy(zz).wait_recv()
                tot[...] += ur[zz].astype(F32)

            @pl.when(z < A - 1)
            def _():
                down_copy(zz).wait_recv()
                tot[...] += dr[zz].astype(F32)

    far_first(along)
    layer = (x_ref[...].astype(F32) + tot[...]).astype(BF16)
    out_ref[...] = layer
    X2[me] = layer
    ssq[...] = jnp.zeros_like(ssq)

    def score(slot):
        wide = X2[slot].astype(F32)
        ssq[...] += jnp.sum(wide * wide, axis=1, keepdims=True)
        piece = (wide * gain2_ref[slot]).astype(BF16)
        acc_l[...] += jnp.dot(piece, lm[slot], preferred_element_type=F32)

    drain2 = gather(X2, ag_s2, ag_r2, score, loads[3].wait)

    logits = jnp.transpose(acc_l[...] * lax.rsqrt(ssq[...] / depth + 1e-05))
    vocab = logits.shape[0]
    word = lax.broadcasted_iota(jnp.int32, logits.shape, 0) + me * vocab
    picked = jnp.sum(jnp.where(word == ids_ref[...], logits, 0.0), axis=0, keepdims=True)
    top = jnp.max(logits, axis=0, keepdims=True)
    total = jnp.sum(jnp.exp(logits - top), axis=0, keepdims=True)
    st[me] = jnp.concatenate([top, total, picked, jnp.zeros((5, tokens), F32)], axis=0)

    def st_copy(slot, i, dev):
        return rc(st.at[slot], st.at[slot], st_s.at[i], st_r.at[slot], dev)

    def st_send(i, carry):
        st_copy(me, i, lax.rem(me + i, n)).start()
        return carry

    lax.fori_loop(1, n, st_send, 0)

    drain1()
    drain2()
    for i in range(users):
        @pl.when(head_of + KVH * i != me)
        def _():
            kv_send(i).wait_send()

    def rs_drain(zz, carry):
        core_copy(0, zz).wait_send()
        core_copy(1, zz).wait_send()
        side_copy(zz).wait_send()

        @pl.when(zz > z)
        def _():
            up_copy(zz).wait_send()

        @pl.when(zz < z)
        def _():
            down_copy(zz).wait_send()

        return carry

    lax.fori_loop(0, A, rs_drain, 0)

    def st_got(i, carry):
        slot = lax.rem(me + i, n)
        st_copy(slot, i, core).wait_recv()
        st_copy(me, i, slot).wait_send()
        return carry

    lax.fori_loop(1, n, st_got, 0)
    parts = st[...]
    tops, totals, hits = parts[:, 0, :], parts[:, 1, :], parts[:, 2, :]
    peak = jnp.max(tops, axis=0, keepdims=True)
    whole = jnp.sum(totals * jnp.exp(tops - peak), axis=0, keepdims=True)
    logp_ref[...] = jnp.sum(hits, axis=0, keepdims=True) - peak - jnp.log(whole)


def body(
    stream, target_ids, lengths, attn_gain, w_query, w_key, w_value, w_out, final_gain, lm_head
):
    tokens, width = stream.shape
    depth = w_query.shape[0]
    n = depth // width
    A = n // (B * C)
    kv_cols, vocab = w_key.shape[1], lm_head.shape[1]
    users, pieces = n // KVH, HD // kv_cols
    cosine, sine = rope_tables(tokens)
    if width % 128:
        w_out = w_out.reshape(HD, n, width).transpose(1, 0, 2)
    vmem = pl.BlockSpec(memory_space=pltpu.VMEM)
    smem = pl.BlockSpec(memory_space=pltpu.SMEM)
    hbm = pl.BlockSpec(memory_space=pl.ANY)
    block = (tokens, width)
    dma = pltpu.SemaphoreType.DMA
    V = pltpu.VMEM
    layer_out, logp = pl.pallas_call(
        functools.partial(kernel, n, depth),
        out_shape=(
            jax.ShapeDtypeStruct(block, BF16),
            jax.ShapeDtypeStruct((1, tokens), F32),
        ),
        in_specs=[vmem, vmem, smem] + [vmem] * 4 + [hbm] * 5,
        out_specs=(vmem, vmem),
        scratch_shapes=[
            V((n, width, HD), BF16), V((n, width, kv_cols), BF16), V((n, width, kv_cols), BF16),
            V((n, HD, width), BF16), V((n, width, vocab), BF16),
            V((n,) + block, BF16), V((n,) + block, BF16),
            V((tokens, HD), F32), V((tokens, kv_cols), F32), V((tokens, kv_cols), F32),
            V((tokens, 1), F32), V((tokens, vocab), F32),
            V((2, tokens, kv_cols), F32), V((pieces, 2, tokens, kv_cols), F32),
            V((tokens, HD), BF16),
            V((2, A) + block, BF16), V((2, A) + block, BF16),
            V((A,) + block, BF16), V((A,) + block, BF16),
            V((A,) + block, BF16), V((A,) + block, BF16),
            V((A,) + block, BF16), V((A,) + block, BF16),
            V(block, F32), V((n, 8, tokens), F32),
            dma((4,)), dma((n,)),
            dma((4, B * A)), dma((n,)), dma((4, B * A)), dma((n,)),
            dma((users,)), dma((pieces,)),
            dma((2, A)), dma((2, A)), dma((A,)), dma((A,)),
            dma((A,)), dma((A,)), dma((A,)), dma((A,)),
            dma((n,)), dma((n,)),
        ],
        compiler_params=pltpu.CompilerParams(
            collective_id=0, has_side_effects=True, vmem_limit_bytes=56 * 1024 * 1024
        ),
        cost_estimate=pl.CostEstimate(
            flops=2 * tokens * depth * (2 * HD + 2 * kv_cols + vocab),
            bytes_accessed=2 * depth * (2 * HD + 2 * kv_cols + vocab),
            transcendentals=0,
        ),
    )(
        stream, target_ids.reshape(1, tokens), lengths,
        attn_gain.reshape(n, 1, width), final_gain.reshape(n, 1, width),
        jnp.asarray(cosine), jnp.asarray(sine),
        w_query.reshape(n, width, HD), w_key.reshape(n, width, kv_cols),
        w_value.reshape(n, width, kv_cols), w_out, lm_head.reshape(n, width, vocab),
    )
    return layer_out, logp.reshape(tokens)


def solution(mesh):
    return jax.shard_map(
        body,
        mesh=mesh,
        in_specs=(
            P("groups", "mp"),
            P("groups"),
            P("groups"),
            P(),
            P(None, "mp"),
            P(None, "mp"),
            P(None, "mp"),
            P("mp", None),
            P(),
            P(None, "mp"),
        ),
        out_specs=(P("groups", "mp"), P("groups")),
        check_vma=False,
    )
```

time: 373 us -> 98.4 us (0.26)
  waiting for transfers between devices: 168 us -> 0 us
  blocking collectives: 164 us -> 0 us
  Pallas kernels: 0 us -> 87.7 us
  matrix products: 17.1 us -> 0 us
  between operations: 13.9 us -> 0.65 us
  local copies, waits for them, and re-layouts: 1.74 us -> 9.81 us
  other arithmetic: 6.78 us -> 0 us
    psum x3 -> x0, blocking collectives: 95.7 us -> none  [the longest x1 34.9 us: body(): sum_sq = lax.psum(jnp.sum(wide * wide, axis=1), 'mp')]
    pallas_call x0 -> x1, Pallas kernels: none -> 87.7 us  [body(): pl.pallas_call(functools.partial(kernel, n, depth), out_shape=(jax.ShapeD...]
    all_gather x2 -> x0, waiting for transfers between devices: 85.1 us -> none  [the longest x1 43 us: body(): lax.all_gather(final_local, 'mp', axis=1, tiled=True)]
    reduce_scatter x1 -> x0, waiting for transfers between devices: 82.9 us -> none  [body(): lax.psum_scatter(lax.dot_general(w_out, attn, (((0,), (1,)), ((), ())), p...]
    all_gather x2 -> x0, blocking collectives: 37.7 us -> none  [the longest x1 19.6 us: body(): lax.all_gather(key_local, 'mp', axis=1, tiled=True)]
    pmax x1 -> x0, blocking collectives: 31.1 us -> none  [body(): top = lax.pmax(part_max, 'mp')]
    dot_general x6 -> x0, matrix products: 17.1 us -> none  [the longest x1 4.8 us: body(): jnp.dot(lax.all_gather(final_local, 'mp', axis=1, tiled=True), lm_head, p...]
    unnamed x12 -> x6, local copies, waits for them, and re-layouts: 0.03 us -> 9.81 us
  transfers between devices with their start and end apart: 3 -> 0, of which waited for: 3 -> 0; matrix products, arithmetic and copies ran while one was open for 0% -> 0% of each run, Pallas kernels for 0% -> 0%
where the time goes in v1:
time: 98.4 us; the launch traced here: 98.2 us
  Pallas kernels  87.7 us (89%)
  local copies, waits for them, and re-layouts  9.81 us (10%)
    pallas_call x1, Pallas kernels, body(): pl.pallas_call(functools.partial(kernel, n, depth), out_shape=(jax.ShapeD...  87.7 us
    unnamed x6, local copies, waits for them, and re-layouts  9.81 us

profile of v1, /device:TPU:0, one launch (start us, length us, event | category | flops | bytes accessed | tf_op | source)
XLA Modules:
  0.0 98.2 jit_solution(2915582177646649548)
XLA Ops:
  0.6 0.0 copy-start
  0.6 4.2 %copy.14 = bf16[12288,64]{1,0:T(8,128)(2,1)} copy(bf16[12288,64]{0,1:T(8,128)(2,1)} %param.17) | data formatting | bytes 3145728 | tf_op args[5]
  4.9 0.0 copy-done
  4.9 2.8 %copy.15 = bf16[12288,64]{1,0:T(8,128)(2,1)} copy(bf16[12288,64]{0,1:T(8,128)(2,1)S(1)} %copy-done) | data formatting | bytes 3145728 | tf_op args[6]
  7.6 87.7 %shard_map.131 = (bf16[128,768]{1,0:T(8,128)(2,1)}, f32[1,128]{1,0:T(1,128)}) custom-call(bf16[128,768]{1,0:T(8,128)(2,1)} %x_ref.1, s32[1,128]{1,0:T(1,128)} %bitcast.14, s32[2]{0:T(128)} %len_ref.1, f32[16,1,768]{2,1,0:T(1,128)} %bitcast.12, f32[16,1,768]{2,1,0:T(1,128)} %bitcast.13, f32[128,128]{1,0:T(8,128)} %constant.4.clone.cos_ref, ...), custom_call_target="tpu_custom_call" | custom-call | flops 2013265920 | bytes 15728640 | tf_op jit(solution)/shard_map/pallas_call | solution.py:446
  95.4 1.6 %copy.18 = bf16[128,768]{1,0:T(8,128)(2,1)} copy(bf16[128,768]{1,0:T(8,128)(2,1)} %get-tuple-element.8) | data formatting | bytes 393216
  97.0 1.2 %copy.19 = f32[128]{0:T(128)} copy(f32[128]{0:T(128)} %bitcast.15) | data formatting | bytes 1024
Async XLA Ops:
  0.6 4.3 %copy-start = (bf16[12288,64]{0,1:T(8,128)(2,1)S(1)}, bf16[12288,64]{0,1:T(8,128)(2,1)}, u32[]{:S(2)}) copy-start(bf16[12288,64]{0,1:T(8,128)(2,1)} %param.18) | copy-start | bytes 4718596

commit v2 on v1

--- a/solution.py
+++ b/solution.py
@@ -36,9 +36,9 @@
     x_ref, ids_ref, len_ref, gain1_ref, gain2_ref, cos_ref, sin_ref,
     wq_hbm, wk_hbm, wv_hbm, wo_hbm, lm_hbm,
     out_ref, logp_ref,
-    wq, wk, wv, wo, lm, X1, X2, acc_q, acc_k, acc_v, ssq, acc_l,
+    wq, wkv, wo, lm, X1, X2, acc_q, acc_kv, ssq, acc_l,
     kvs, kvr, attn, cs, cr, ys, yr, us, ur, ds, dr, tot, st,
-    wsem, wosem, ag_s1, ag_r1, ag_s2, ag_r2, kv_s, kv_r,
+    wsem, wkvsem, wosem, ag_s1, ag_r1, ag_s2, ag_r2, kv_s, kv_r,
     cs_s, cs_r, ys_s, ys_r, us_s, us_r, ds_s, ds_r, st_s, st_r,
 ):
     A = n // (B * C)
@@ -47,7 +47,7 @@
     y = lax.rem(lax.div(me, C), B)
     z = lax.div(me, B * C)
     tokens, width = x_ref.shape
-    kv_cols = wk.shape[2]
+    kv_cols = wkv.shape[1] // 2
     pieces = HD // kv_cols
     users = n // KVH
 
@@ -63,14 +63,21 @@
             device_id={"mp": dev}, device_id_type=pl.DeviceIdType.MESH,
         )
 
-    loads = [
-        pltpu.make_async_copy(src, dst, wsem.at[i])
-        for i, (src, dst) in enumerate(((wq_hbm, wq), (wk_hbm, wk), (wv_hbm, wv), (lm_hbm, lm)))
-    ]
+    def columns(ref, j):
+        return ref.at[j] if len(ref.shape) == 3 else ref.at[:, j * width:(j + 1) * width]
+
+    q_load = pltpu.make_async_copy(wq_hbm, wq, wsem.at[0])
+    lm_load = pltpu.make_async_copy(lm_hbm, lm, wsem.at[1])
+
+    def kv_load(i, j):
+        return pltpu.make_async_copy(
+            columns((wk_hbm, wv_hbm)[i], j),
+            wkv.at[j, i * kv_cols:(i + 1) * kv_cols],
+            wkvsem.at[i, j],
+        )
 
     def wo_load(j):
-        src = wo_hbm.at[j] if len(wo_hbm.shape) == 3 else wo_hbm.at[:, j * width:(j + 1) * width]
-        return pltpu.make_async_copy(src, wo.at[j], wosem.at[j])
+        return pltpu.make_async_copy(columns(wo_hbm, j), wo.at[j], wosem.at[j])
 
     barrier = pltpu.get_barrier_semaphore()
 
@@ -81,12 +88,13 @@
         return carry
 
     lax.fori_loop(1, n, greet, 0)
-    for load in loads[:3]:
-        load.start()
+    q_load.start()
+    for j in range(n):
+        kv_load(0, j).start()
+        kv_load(1, j).start()
     X1[me] = x_ref[...]
     acc_q[...] = jnp.zeros_like(acc_q)
-    acc_k[...] = jnp.zeros_like(acc_k)
-    acc_v[...] = jnp.zeros_like(acc_v)
+    acc_kv[...] = jnp.zeros_like(acc_kv)
     acc_l[...] = jnp.zeros_like(acc_l)
     ssq[...] = jnp.zeros_like(ssq)
     pl.semaphore_wait(barrier, n - 1)
@@ -206,21 +214,22 @@
         ssq[...] += jnp.sum(wide * wide, axis=1, keepdims=True)
         piece = (wide * gain1_ref[slot]).astype(BF16)
         acc_q[...] += jnp.dot(piece, wq[slot], preferred_element_type=F32)
-        acc_k[...] += jnp.dot(piece, wk[slot], preferred_element_type=F32)
-        acc_v[...] += jnp.dot(piece, wv[slot], preferred_element_type=F32)
+        acc_kv[...] += lax.dot_general(
+            piece, wkv[slot], (((1,), (1,)), ((), ())), preferred_element_type=F32
+        )
 
     def ready():
-        for load in loads[:3]:
-            load.wait()
+        q_load.wait()
         for j in range(n):
+            kv_load(0, j).wait()
+            kv_load(1, j).wait()
             wo_load(j).start()
-        loads[3].start()
+        lm_load.start()
 
     drain1 = gather(X1, ag_s1, ag_r1, project, ready)
 
     scale = lax.rsqrt(ssq[...] / depth + 1e-05)
-    kvs[0] = acc_k[...] * scale
-    kvs[1] = acc_v[...] * scale
+    kvs[...] = acc_kv[...] * scale
     piece_id, head_of = lax.rem(me, pieces), lax.div(me, pieces)
 
     def kv_send(i):
@@ -243,9 +252,9 @@
         def _():
             rc(kvs, kvr.at[i], kv_s.at[0], kv_r.at[i], core).wait_recv()
 
-    key = jnp.concatenate([kvr[i, 0] for i in range(pieces)], axis=1)
+    key = jnp.concatenate([kvr[i, :, :kv_cols] for i in range(pieces)], axis=1)
     key = rope(key, cosine, sine).astype(BF16)
-    value = jnp.concatenate([kvr[i, 1] for i in range(pieces)], axis=1).astype(BF16)
+    value = jnp.concatenate([kvr[i, :, kv_cols:] for i in range(pieces)], axis=1).astype(BF16)
     seq_len = tokens // SEQS
     row = lax.broadcasted_iota(jnp.int32, (tokens, tokens), 0)
     col = lax.broadcasted_iota(jnp.int32, (tokens, tokens), 1)
@@ -368,7 +377,7 @@
         piece = (wide * gain2_ref[slot]).astype(BF16)
         acc_l[...] += jnp.dot(piece, lm[slot], preferred_element_type=F32)
 
-    drain2 = gather(X2, ag_s2, ag_r2, score, loads[3].wait)
+    drain2 = gather(X2, ag_s2, ag_r2, score, lm_load.wait)
 
     logits = jnp.transpose(acc_l[...] * lax.rsqrt(ssq[...] / depth + 1e-05))
     vocab = logits.shape[0]
@@ -435,8 +444,10 @@
     kv_cols, vocab = w_key.shape[1], lm_head.shape[1]
     users, pieces = n // KVH, HD // kv_cols
     cosine, sine = rope_tables(tokens)
+    across = [w_key.T, w_value.T, w_out]
     if width % 128:
-        w_out = w_out.reshape(HD, n, width).transpose(1, 0, 2)
+        across = [w.reshape(-1, n, width).transpose(1, 0, 2) for w in across]
+    wk_t, wv_t, w_out = across
     vmem = pl.BlockSpec(memory_space=pltpu.VMEM)
     smem = pl.BlockSpec(memory_space=pltpu.SMEM)
     hbm = pl.BlockSpec(memory_space=pl.ANY)
@@ -452,19 +463,19 @@
         in_specs=[vmem, vmem, smem] + [vmem] * 4 + [hbm] * 5,
         out_specs=(vmem, vmem),
         scratch_shapes=[
-            V((n, width, HD), BF16), V((n, width, kv_cols), BF16), V((n, width, kv_cols), BF16),
+            V((n, width, HD), BF16), V((n, 2 * kv_cols, width), BF16),
             V((n, HD, width), BF16), V((n, width, vocab), BF16),
             V((n,) + block, BF16), V((n,) + block, BF16),
-            V((tokens, HD), F32), V((tokens, kv_cols), F32), V((tokens, kv_cols), F32),
+            V((tokens, HD), F32), V((tokens, 2 * kv_cols), F32),
             V((tokens, 1), F32), V((tokens, vocab), F32),
-            V((2, tokens, kv_cols), F32), V((pieces, 2, tokens, kv_cols), F32),
+            V((tokens, 2 * kv_cols), F32), V((pieces, tokens, 2 * kv_cols), F32),
             V((tokens, HD), BF16),
             V((2, A) + block, BF16), V((2, A) + block, BF16),
             V((A,) + block, BF16), V((A,) + block, BF16),
             V((A,) + block, BF16), V((A,) + block, BF16),
             V((A,) + block, BF16), V((A,) + block, BF16),
             V(block, F32), V((n, 8, tokens), F32),
-            dma((4,)), dma((n,)),
+            dma((2,)), dma((2, n)), dma((n,)),
             dma((4, B * A)), dma((n,)), dma((4, B * A)), dma((n,)),
             dma((users,)), dma((pieces,)),
             dma((2, A)), dma((2, A)), dma((A,)), dma((A,)),
@@ -483,8 +494,7 @@
         stream, target_ids.reshape(1, tokens), lengths,
         attn_gain.reshape(n, 1, width), final_gain.reshape(n, 1, width),
         jnp.asarray(cosine), jnp.asarray(sine),
-        w_query.reshape(n, width, HD), w_key.reshape(n, width, kv_cols),
-        w_value.reshape(n, width, kv_cols), w_out, lm_head.reshape(n, width, vocab),
+        w_query.reshape(n, width, HD), wk_t, wv_t, w_out, lm_head.reshape(n, width, vocab),
     )
     return layer_out, logp.reshape(tokens)
 

time: 98.4 us -> 90.3 us (0.918)
  local copies, waits for them, and re-layouts: 9.81 us -> 2.75 us
  Pallas kernels: 87.7 us -> 86.7 us
    unnamed x6 -> x2, local copies, waits for them, and re-layouts: 9.81 us -> 2.75 us
    pallas_call x1, Pallas kernels: 87.7 us -> 86.7 us  [body(): pl.pallas_call(functools.partial(kernel, n, depth), out_shape=(jax.ShapeD...]
where the time goes in v2:
time: 90.3 us; the launch traced here: 90.1 us
  Pallas kernels  86.7 us (96%)
  local copies, waits for them, and re-layouts  2.75 us (3%)
    pallas_call x1, Pallas kernels, body(): pl.pallas_call(functools.partial(kernel, n, depth), out_shape=(jax.ShapeD...  86.7 us
    unnamed x2, local copies, waits for them, and re-layouts  2.75 us

profile of v2, /device:TPU:0, one launch (start us, length us, event | category | flops | bytes accessed | tf_op | source)
XLA Modules:
  0.0 90.1 jit_solution(8650028273185482642)
XLA Ops:
  0.6 86.7 %shard_map.131 = (bf16[128,768]{1,0:T(8,128)(2,1)}, f32[1,128]{1,0:T(1,128)}) custom-call(bf16[128,768]{1,0:T(8,128)(2,1)} %x_ref.1, s32[1,128]{1,0:T(1,128)} %bitcast.14, s32[2]{0:T(128)} %len_ref.1, f32[16,1,768]{2,1,0:T(1,128)} %bitcast.12, f32[16,1,768]{2,1,0:T(1,128)} %bitcast.13, f32[128,128]{1,0:T(8,128)} %constant.4.clone.cos_ref, ...), custom_call_target="tpu_custom_call" | custom-call | flops 2013265920 | bytes 15728640 | tf_op jit(solution)/shard_map/pallas_call | solution.py:457
  87.4 1.6 %copy.16 = bf16[128,768]{1,0:T(8,128)(2,1)} copy(bf16[128,768]{1,0:T(8,128)(2,1)} %get-tuple-element.8) | data formatting | bytes 393216
  89.0 1.1 %copy.17 = f32[128]{0:T(128)} copy(f32[128]{0:T(128)} %bitcast.15) | data formatting | bytes 1024

commit v3 on v2

--- a/solution.py
+++ b/solution.py
@@ -12,6 +12,7 @@
 HD = 128
 SEQS = 2
 B, C = 2, 2
+HALVES = 2
 BF16, F32 = jnp.bfloat16, jnp.float32
 
 
@@ -100,22 +101,27 @@
     pl.semaphore_wait(barrier, n - 1)
 
     def gather(X, ss, rs, consume, prepare):
-        def send(slot, kind, k, dev):
-            return rc(X.at[slot], X.at[slot], ss.at[kind, k], rs.at[slot], dev)
-
-        def got(slot):
-            rc(X.at[slot], X.at[slot], ss.at[0, 0], rs.at[slot], core).wait_recv()
-
-        @pl.when(z < A - 1)
-        def _():
-            send(me, 0, z, above).start()
-
-        @pl.when(z > 0)
-        def _():
-            send(me, 1, z, below).start()
-
-        send(me, 2, z, side).start()
-        send(me, 3, z * B + y, core).start()
+        rows = tokens // HALVES
+
+        def send(slot, kind, k, dev, h):
+            view = X.at[slot, h * rows:(h + 1) * rows]
+            return rc(view, view, ss.at[h, kind, k], rs.at[h, slot], dev)
+
+        def got(slot, h):
+            send(slot, 0, 0, core, h).wait_recv()
+
+        for h in range(HALVES):
+            @pl.when(z < A - 1)
+            def _():
+                send(me, 0, z, above, h).start()
+
+            @pl.when(z > 0)
+            def _():
+                send(me, 1, z, below, h).start()
+
+            send(me, 2, z, side, h).start()
+        for h in range(HALVES):
+            send(me, 3, z * B + y, core, h).start()
         prepare()
         consume(me)
 
@@ -129,18 +135,19 @@
                 @pl.when(valid(s, g, zz))
                 def _():
                     slot = idx(zz, y, c)
-                    got(slot)
-
-                    @pl.when((g == 0) & (z < A - 1))
-                    def _():
-                        send(slot, 0, zz, above).start()
-
-                    @pl.when((g == 1) & (z > 0))
-                    def _():
-                        send(slot, 1, zz, below).start()
-
-                    send(slot, 2, zz, side).start()
-                    send(slot, 3, zz * B + y, core).start()
+                    for h in range(HALVES):
+                        got(slot, h)
+
+                        @pl.when((g == 0) & (z < A - 1))
+                        def _():
+                            send(slot, 0, zz, above, h).start()
+
+                        @pl.when((g == 1) & (z > 0))
+                        def _():
+                            send(slot, 1, zz, below, h).start()
+
+                        send(slot, 2, zz, side, h).start()
+                        send(slot, 3, zz * B + y, core, h).start()
 
                 return carry
 
@@ -163,11 +170,13 @@
                 @pl.when(valid(s - 1, g, zz))
                 def _():
                     slot = idx(zz, 1 - y, c)
-                    got(slot)
-                    send(slot, 3, zz * B + 1 - y, core).start()
+                    for h in range(HALVES):
+                        got(slot, h)
+                        send(slot, 3, zz * B + 1 - y, core, h).start()
                     consume(slot)
                     slot2 = idx(zz, y, 1 - c)
-                    got(slot2)
+                    for h in range(HALVES):
+                        got(slot2, h)
                     consume(slot2)
 
                 return carry
@@ -180,7 +189,8 @@
                 @pl.when(valid(s - 2, g, zz))
                 def _():
                     slot = idx(zz, 1 - y, 1 - c)
-                    got(slot)
+                    for h in range(HALVES):
+                        got(slot, h)
                     consume(slot)
 
                 return carry
@@ -193,18 +203,19 @@
         def drain(zz, carry):
             slot = idx(zz, y, c)
 
-            @pl.when((zz <= z) & (z < A - 1))
-            def _():
-                send(slot, 0, zz, above).wait_send()
-
-            @pl.when((zz >= z) & (z > 0))
-            def _():
-                send(slot, 1, zz, below).wait_send()
-
-            send(slot, 2, zz, side).wait_send()
-            send(slot, 3, zz * B + y, core).wait_send()
             other = idx(zz, 1 - y, c)
-            send(other, 3, zz * B + 1 - y, core).wait_send()
+            for h in range(HALVES):
+                @pl.when((zz <= z) & (z < A - 1))
+                def _():
+                    send(slot, 0, zz, above, h).wait_send()
+
+                @pl.when((zz >= z) & (z > 0))
+                def _():
+                    send(slot, 1, zz, below, h).wait_send()
+
+                send(slot, 2, zz, side, h).wait_send()
+                send(slot, 3, zz * B + y, core, h).wait_send()
+                send(other, 3, zz * B + 1 - y, core, h).wait_send()
             return carry
 
         return lambda: lax.fori_loop(0, A, drain, 0)
@@ -476,7 +487,7 @@
             V((A,) + block, BF16), V((A,) + block, BF16),
             V(block, F32), V((n, 8, tokens), F32),
             dma((2,)), dma((2, n)), dma((n,)),
-            dma((4, B * A)), dma((n,)), dma((4, B * A)), dma((n,)),
+            dma((HALVES, 4, B * A)), dma((HALVES, n)), dma((HALVES, 4, B * A)), dma((HALVES, n)),
             dma((users,)), dma((pieces,)),
             dma((2, A)), dma((2, A)), dma((A,)), dma((A,)),
             dma((A,)), dma((A,)), dma((A,)), dma((A,)),

time: 90.3 us -> 85.7 us (0.949)
  Pallas kernels: 86.7 us -> 82.1 us
    pallas_call x1, Pallas kernels: 86.7 us -> 82.1 us  [body(): pl.pallas_call(functools.partial(kernel, n, depth), out_shape=(jax.ShapeD...]
where the time goes in v3:
time: 85.7 us; the launch traced here: 85.5 us
  Pallas kernels  82.1 us (96%)
  local copies, waits for them, and re-layouts  2.75 us (3%)
    pallas_call x1, Pallas kernels, body(): pl.pallas_call(functools.partial(kernel, n, depth), out_shape=(jax.ShapeD...  82.1 us
    unnamed x2, local copies, waits for them, and re-layouts  2.75 us

profile of v3, /device:TPU:0, one launch (start us, length us, event | category | flops | bytes accessed | tf_op | source)
XLA Modules:
  0.0 85.5 jit_solution(11422682585600440875)
XLA Ops:
  0.6 82.1 %shard_map.131 = (bf16[128,768]{1,0:T(8,128)(2,1)}, f32[1,128]{1,0:T(1,128)}) custom-call(bf16[128,768]{1,0:T(8,128)(2,1)} %x_ref.1, s32[1,128]{1,0:T(1,128)} %bitcast.14, s32[2]{0:T(128)} %len_ref.1, f32[16,1,768]{2,1,0:T(1,128)} %bitcast.12, f32[16,1,768]{2,1,0:T(1,128)} %bitcast.13, f32[128,128]{1,0:T(8,128)} %constant.4.clone.cos_ref, ...), custom_call_target="tpu_custom_call" | custom-call | flops 2013265920 | bytes 15728640 | tf_op jit(solution)/shard_map/pallas_call | solution.py:468
  82.7 1.6 %copy.16 = bf16[128,768]{1,0:T(8,128)(2,1)} copy(bf16[128,768]{1,0:T(8,128)(2,1)} %get-tuple-element.8) | data formatting | bytes 393216
  84.4 1.1 %copy.17 = f32[128]{0:T(128)} copy(f32[128]{0:T(128)} %bitcast.15) | data formatting | bytes 1024
